TPU v7x, 512 devices: a whole 4x4x16 slice. The times are simulated.
512 devices in a mesh: dp: 16 (over y, x), tensor: 32 (over z, core).
Axes of the slice: x: 4, y: 4, z: 16, core: 2. Of those that a mesh axis runs over, the one named last changes fastest.
Arguments:
- activations: bfloat16 [2048, 8192], P('dp'), may hold values from -6 to 6
- cotangent: bfloat16 [2, 2048, 28672], P(None, 'dp', 'tensor'), may hold values from -6 to 6
- weights: bfloat16 [2, 8192, 28672], P(None, 'dp', 'tensor'), may hold values from -0.0625 to 0.0625
- proj_basis: bfloat16 [8192, 512], replicated, may hold values from -0.0625 to 0.0625
- first_moment: float32 [2, 512, 28672], P(None, 'dp', 'tensor'), may hold values from -6 to 6
- second_moment: float32 [2, 512, 28672], P(None, 'dp', 'tensor'), may hold values from 1 to 20
- step_number: int32 [1], replicated, may hold values from 1 to 999
Outputs:
- input_grad: bfloat16 [2048, 8192], P(None, 'dp')
- update: bfloat16 [2, 8192, 28672], P(None, 'dp', 'tensor')
- first_new: float32 [2, 512, 28672], P(None, 'dp', 'tensor')
- second_new: float32 [2, 512, 28672], P(None, 'dp', 'tensor')
All inputs are finite; a program needn't handle non-finite values.
Results may differ from a plain program's by a relative error of at most 0.0051.
Values may be sent and summed in bfloat16 or wider, within the bound.
A program may use at most 128 MiB of HBM per device.

v0:
```python
import jax
import jax.numpy as jnp
from jax import lax
from jax.sharding import PartitionSpec as P

beta_one = 0.9
beta_two = 0.999
adam_eps = 1e-08


def adam_moments(projected, first_moment, second_moment, step_number):
    step_value = step_number[0].astype(jnp.float32)
    first_new = beta_one * first_moment + (1.0 - beta_one) * projected
    second_new = beta_two * second_moment + (1.0 - beta_two) * projected * projected
    first_fix = 1.0 - jnp.power(jnp.float32(beta_one), step_value)
    second_fix = 1.0 - jnp.power(jnp.float32(beta_two), step_value)
    normalized = first_new / first_fix / (jnp.sqrt(second_new / second_fix) + adam_eps)
    return (first_new, second_new, normalized)


def local(activations, cotangent, weights, proj_basis, first_moment, second_moment, step_number):
    gathered = lax.all_gather(cotangent, "dp", axis=1, tiled=True)
    local_terms = jnp.einsum("gtf,gdf->td", gathered, weights, preferred_element_type=jnp.float32)
    input_grad = lax.psum(local_terms, "tensor").astype(jnp.bfloat16)
    coords = jnp.dot(activations, proj_basis, preferred_element_type=jnp.float32).astype(
        jnp.bfloat16
    )
    dp_index = lax.axis_index("dp")
    partial_sums = jnp.einsum("tr,gtf->grf", coords, cotangent, preferred_element_type=jnp.float32)
    projected = lax.psum_scatter(partial_sums, "dp", scatter_dimension=1, tiled=True)
    first_new, second_new, normalized = adam_moments(
        projected, first_moment, second_moment, step_number
    )
    full_normal = lax.all_gather(normalized, "dp", axis=1, tiled=True)
    weight_rows = weights.shape[1]
    basis_rows = lax.dynamic_slice_in_dim(
        proj_basis, dp_index * weight_rows, weight_rows, 0
    ).astype(jnp.float32)
    update = jnp.einsum(
        "dr,grf->gdf", basis_rows, full_normal, precision=lax.Precision.HIGHEST
    ).astype(jnp.bfloat16)
    return (input_grad, update, first_new, second_new)


def solution(mesh):
    return jax.shard_map(
        local,
        mesh=mesh,
        in_specs=(
            P("dp", None),
            P(None, "dp", "tensor"),
            P(None, "dp", "tensor"),
            P(),
            P(None, "dp", "tensor"),
            P(None, "dp", "tensor"),
            P(),
        ),
        out_specs=(
            P(None, "dp"),
            P(None, "dp", "tensor"),
            P(None, "dp", "tensor"),
            P(None, "dp", "tensor"),
        ),
        check_vma=False,
    )
```

profile of v0, /device:TPU:1, one launch (start us, length us, event | category | flops | bytes accessed | tf_op | source)
XLA Modules:
  0.0 345.4 jit_solution(11938657067657961840)
XLA Ops:
  7.2 0.0 copy-start
  7.2 0.0 reduce-scatter.2.cloned.1.call-start
  7.2 1.5 copy-done
  8.8 9.4 %convolution_bitcast_fusion.1 = f32[2,512,896]{2,1,0:T(8,128)} fusion(bf16[2,128,896]{2,1,0:T(8,128)(2,1)} %param.8, bf16[128,8192]{1,0:T(8,128)(2,1)S(1)} %copy-done, bf16[8192,512]{1,0:T(8,128)(2,1)} %param.10), kind=kOutput, calls=%fused_computation.1 | convolution fusion | flops 1308688384 | bytes 14614528 | tf_op jit(solution)/shard_map/tr,gtf->grf/dot_general | solution.py:29
  18.1 0.0 copy-start.1
  18.2 0.0 copy-start.2
  18.2 0.0 reduce-scatter.2.cloned.1.call-update
  18.2 0.0 all-gather.3.cloned.1.call-start
  18.2 0.7 all-gather.3.cloned.1.call-update
  18.9 0.0 all-gather.5.cloned.1.call-start
  19.7 94.1 %reduce-scatter.2.cloned.1.call-done = f32[2,32,896]{2,1,0:T(8,128)} async-done(((f32[2,512,896]{2,1,0:T(8,128)}), f32[2,32,896]{2,1,0:T(8,128)}) %reduce-scatter.2.cloned.1.call-update) | async-done | bytes 229392 | tf_op jit(solution)/shard_map/reduce_scatter | solution.py:30
  113.8 0.0 copy-done.1
  113.8 0.0 copy-done.2
  113.8 1.8 multiply_divide_fusion
  115.6 0.0 all-gather.5.cloned.1.call-update
  115.7 83.7 %all-gather.3.cloned.1.call-done = bf16[2,2048,896]{2,1,0:T(8,128)(2,1)} async-done(((bf16[2,128,896]{2,1,0:T(8,128)(2,1)}), bf16[2,2048,896]{2,1,0:T(8,128)(2,1)}) %all-gather.3.cloned.1.call-update) | async-done | bytes 7340048 | tf_op jit(solution)/shard_map/all_gather | solution.py:22
  199.4 9.7 %convolution_bitcast_fusion = f32[2048,512]{1,0:T(8,128)} fusion(bf16[2,2048,896]{2,1,0:T(8,128)(2,1)} %all-gather.3.cloned.1.call-done, bf16[2,512,896]{2,1,0:T(8,128)(2,1)} %param.9), kind=kOutput, calls=%fused_computation | convolution fusion | flops 3758096384 | bytes 13369344 | tf_op jit(solution)/shard_map/gtf,gdf->td/dot_general | solution.py:23
  209.0 117.0 %all-reduce.1 = bf16[2048,512]{1,0:T(8,128)(2,1)} all-reduce(f32[2048,512]{1,0:T(8,128)} %convolution_bitcast_fusion), channel_id=1, replica_groups=mesh['dp'=16,'tensor'=32] {'tensor'}, use_global_device_ids=true, to_apply=%region_0.0 | all-reduce | flops 1048576 | bytes 6291456 | tf_op jit(solution)/shard_map/psum | solution.py:24
  326.0 0.0 all-gather.5.cloned.1.call-done
  326.0 9.3 %convert_bitcast_fusion = bf16[2,512,896]{1,2,0:T(8,128)(2,1)} fusion(f32[2,512,896]{2,1,0:T(8,128)} %all-gather.5.cloned.1.call-done, bf16[8192,512]{1,0:T(8,128)(2,1)} %param.10, s32[]{:T(128)S(6)} %select_n.3), kind=kOutput, calls=%fused_computation.2 | convolution fusion | flops 5638062080 | bytes 6029316 | tf_op jit(solution)/shard_map/dr,grf->gdf/dot_general | solution.py:39
  335.3 3.5 %copy.11 = bf16[2,512,896]{2,1,0:T(8,128)(2,1)} copy(bf16[2,512,896]{1,2,0:T(8,128)(2,1)} %convert_bitcast_fusion) | data formatting | bytes 3670016
Async XLA Ops:
  7.2 1.6 copy-start
  7.2 106.6 %reduce-scatter.2.cloned.1.call-start = ((), (), s32[]{:S(2)}) async-start(), calls=%async_computation.2 | async-start | bytes 3899392 | tf_op jit(solution)/shard_map/reduce_scatter | solution.py:30
  18.1 95.7 %copy-start.1 = (f32[2,32,896]{2,1,0:T(8,128)S(1)}, f32[2,32,896]{2,1,0:T(8,128)}, u32[]{:S(2)}) copy-start(f32[2,32,896]{2,1,0:T(8,128)} %param.12) | copy-start | bytes 688132
  18.2 95.7 %copy-start.2 = (f32[2,32,896]{2,1,0:T(8,128)S(1)}, f32[2,32,896]{2,1,0:T(8,128)}, u32[]{:S(2)}) copy-start(f32[2,32,896]{2,1,0:T(8,128)} %param.11) | copy-start | bytes 688132
  18.2 181.2 %all-gather.3.cloned.1.call-start = ((), (), s32[]{:S(2)}) async-start(), calls=%async_computation.1 | async-start | bytes 7798784 | tf_op jit(solution)/shard_map/all_gather | solution.py:22
  18.9 307.1 %all-gather.5.cloned.1.call-start = ((), (), s32[]{:S(2)}) async-start(), calls=%async_computation.3 | async-start | bytes 3899392 | tf_op jit(solution)/shard_map/all_gather | solution.py:34
Sparse Core Ops, SparseCore 0:
  18.3 95.4 reduce-scatter.1
  116.8 82.4 all-gather.2
  202.9 64.3 all-gather.4
where the time goes:
time: 348 us; the launch traced here: 345 us
  waiting for transfers between devices  178 us (51%)
  blocking collectives  117 us (34%)
  matrix products  28.3 us (8%)
  between operations  14.5 us (4%)
  local copies, waits for them, and re-layouts  5.09 us (1%)
    psum x1, blocking collectives, local(): input_grad = lax.psum(local_terms, 'tensor').astype(jnp.bfloat16)  117 us
    reduce_scatter x1, waiting for transfers between devices, local(): lax.psum_scatter(partial_sums, 'dp', scatter_dimension=1, tiled=True)  94.1 us
    all_gather x1, waiting for transfers between devices, local(): gathered = lax.all_gather(cotangent, 'dp', axis=1, tiled=True)  83.7 us
    dot_general x1, matrix products, local(): jnp.einsum('gtf,gdf->td', gathered, weights, preferred_element_type=jnp.f...  9.68 us
    dot_general x1, matrix products, local(): jnp.einsum('tr,gtf->grf', coords, cotangent, preferred_element_type=jnp.f...  9.39 us
    dot_general x1, matrix products, local(): jnp.einsum('dr,grf->gdf', basis_rows, full_normal, precision=lax.Precisio...  9.26 us
  transfers between devices with their start and end apart: 3, of which 2 were waited for; matrix products, arithmetic and copies ran while one was open for 3% of the time, Pallas kernels for 0%

commit v1 on v0

v1 whole, which is shorter than its diff:
```python
import functools
import math

import jax
import jax.numpy as jnp
from jax import lax
from jax.experimental import pallas as pl
from jax.experimental.pallas import tpu as pltpu
from jax.sharding import PartitionSpec as P

MESH = pl.DeviceIdType.MESH
beta_one = 0.9
beta_two = 0.999
adam_eps = 1e-08

F32 = jnp.float32
BF16 = jnp.bfloat16

ROUNDS = (
    ((0, 0), (0, 1), (0, 3), (0, 2)),
    ((1, 0), (3, 0), (2, 0), (1, 1)),
    ((1, 3), (3, 1), (3, 3), (1, 2)),
    ((3, 2), (2, 1), (2, 3), (2, 2)),
)


def remote(src, dst, send, recv, dev):
    return pltpu.make_async_remote_copy(
        src_ref=src, dst_ref=dst, send_sem=send, recv_sem=recv, device_id=dev, device_id_type=MESH
    )


class Gather:
    def __init__(self, buf, full, half, send_full, send_half, x, y):
        self.buf, self.full, self.half = buf, full, half
        self.send_full, self.send_half = send_full, send_half
        self.x, self.y = x, y
        self.rows = buf.shape[2] // 2
        self.sent = []

    def piece(self, g, u, v):
        dy, dx = (v, u) if g == 0 else (u, v)
        return lax.rem(self.y + dy, 4) * 4 + lax.rem(self.x + dx, 4)

    def device(self, g, axis, delta):
        along_x = (axis == 1) == (g == 0)
        if along_x:
            return {"dp": self.y * 4 + lax.rem(self.x + delta, 4)}
        return {"dp": lax.rem(self.y + delta, 4) * 4 + self.x}

    def send(self, g, axis, u, v, delta):
        p = self.piece(g, u, v)
        slot = 0 if axis == 1 else 1 + u
        ref = self.buf.at[g, p]
        copy = remote(
            ref, ref, self.send_full.at[g, slot, delta // 2], self.full.at[g, p],
            self.device(g, axis, delta),
        )
        copy.start()
        self.sent.append(copy)

    def relay(self, g, axis, u, v):
        off = u if axis == 1 else v
        delta, h = (3, 1) if off == 1 else (1, 0)
        p = self.piece(g, u, v)
        slot = 0 if axis == 1 else 1 + u
        ref = self.buf.at[g, p, pl.ds(h * self.rows, self.rows)]
        copy = remote(
            ref, ref, self.send_half.at[g, slot, h], self.half.at[g, p, h],
            self.device(g, axis, delta),
        )
        copy.start()
        self.sent.append(copy)

    def wait_full(self, g, u, v):
        p = self.piece(g, u, v)
        ref = self.buf.at[g, p]
        remote(
            ref, ref, self.send_full.at[g, 0, 0], self.full.at[g, p], self.device(g, 1, 1)
        ).wait_recv()

    def wait_halves(self, g, u, v):
        p = self.piece(g, u, v)
        for h in (0, 1):
            ref = self.buf.at[g, p, pl.ds(h * self.rows, self.rows)]
            remote(
                ref, ref, self.send_half.at[g, 0, 0], self.half.at[g, p, h], self.device(g, 1, 1)
            ).wait_recv()

    def start(self):
        for axis in (1, 2):
            for g in (0, 1):
                for delta in (1, 3):
                    self.send(g, axis, 0, 0, delta)

    def near(self):
        for u in (1, 3):
            for g in (0, 1):
                self.wait_full(g, u, 0)
                self.relay(g, 1, u, 0)
            for g in (0, 1):
                self.wait_full(g, 0, u)
                self.relay(g, 2, 0, u)
            for g in (0, 1):
                for delta in (1, 3):
                    self.send(g, 2, u, 0, delta)

    def far(self):
        for g in (0, 1):
            self.wait_halves(g, 2, 0)
            for delta in (1, 3):
                self.send(g, 2, 2, 0, delta)
        for g in (0, 1):
            self.wait_halves(g, 0, 2)

    def cross(self, u):
        for v in (1, 3):
            for g in (0, 1):
                self.wait_full(g, u, v)
                self.relay(g, 2, u, v)

    def rest(self, u):
        for g in (0, 1):
            self.wait_halves(g, u, 2)

    def drain(self):
        for copy in self.sent:
            copy.wait_send()


def pick(index, values):
    out = values[0]
    for i in range(1, len(values)):
        out = jnp.where(index == i, values[i], out)
    return out


def kernel(
    act_h, cot_h, w_h, basis_h, m1_h, m2_h, step_s,
    ig_h, upd_h, fn_h, sn_h,
    act, basis, w, m1, m2, cot, ct_own, ct, norm, acc, tmp, kept, sib_s, sib_r,
    a_s, a_r, b_s, b_r, out, ig, upd,
    load_sem, ct_send, ct_recv, c_full, c_half, c_sf, c_sh, n_full, n_half, n_sf, n_sh,
    sib_ss, sib_rs, za_s, za_r, zb_s, zb_r, zc_s, zc_r, zd_s, zd_r, ze_s, ze_r, store_sem,
):
    dp = lax.axis_index("dp")
    tensor = lax.axis_index("tensor")
    y, x = lax.div(dp, 4), lax.rem(dp, 4)
    z, c = lax.div(tensor, 2), lax.rem(tensor, 2)
    oc = 1 - c
    r0, q0 = lax.rem(z, 4), lax.div(z, 4)

    def along_z(delta):
        return {"tensor": lax.rem(z + delta + 16, 16) * 2 + c}

    sibling = {"tensor": z * 2 + oc}

    loads = [
        pltpu.make_async_copy(cot_h.at[0], cot.at[0, dp], load_sem.at[0]),
        pltpu.make_async_copy(cot_h.at[1], cot.at[1, dp], load_sem.at[1]),
        pltpu.make_async_copy(act_h, act, load_sem.at[2]),
        pltpu.make_async_copy(basis_h, basis, load_sem.at[3]),
        pltpu.make_async_copy(w_h, w, load_sem.at[4]),
        pltpu.make_async_copy(m1_h, m1, load_sem.at[5]),
        pltpu.make_async_copy(m2_h, m2, load_sem.at[6]),
    ]
    for load in loads:
        load.start()

    barrier = pltpu.get_barrier_semaphore()

    def greet(d, carry):
        pl.semaphore_signal(
            barrier, inc=1, device_id={"dp": lax.rem(dp + d, 16)}, device_id_type=MESH
        )
        return carry

    lax.fori_loop(1, 16, greet, 0)
    for delta in (1, -1, 2, -2, 4, -4, 8):
        pl.semaphore_signal(barrier, inc=1, device_id=along_z(delta), device_id_type=MESH)
    pl.semaphore_signal(barrier, inc=1, device_id=sibling, device_id_type=MESH)
    pl.semaphore_wait(barrier, 23)

    gather = Gather(cot, c_full, c_half, c_sf, c_sh, x, y)
    loads[0].wait()
    loads[1].wait()
    gather.start()

    loads[2].wait()
    loads[3].wait()

    def coord_step(i, total):
        cols = pl.ds(pl.multiple_of(i * 1024, 1024), 1024)
        return total + jnp.dot(act[:, cols], basis[cols, :], preferred_element_type=F32)

    coords = lax.fori_loop(0, 8, coord_step, jnp.zeros((128, 512), F32))
    ct_own[...] = coords.T.astype(BF16)

    def ct_copy(d):
        to = lax.rem(dp + d, 16)
        rows = pl.ds(pl.multiple_of(to * 32, 32), 32)
        return remote(ct_own.at[rows], ct.at[dp], ct_send.at[d], ct_recv.at[dp], {"dp": to})

    def ct_start(d, carry):
        ct_copy(d).start()
        return carry

    lax.fori_loop(1, 16, ct_start, 0)
    ct[dp] = ct_own[pl.ds(pl.multiple_of(dp * 32, 32), 32), :]

    gather.near()

    def ct_wait(d, carry):
        s = lax.rem(dp + d, 16)
        remote(ct.at[s], ct.at[s], ct_send.at[d], ct_recv.at[s], {"dp": s}).wait_recv()
        return carry

    lax.fori_loop(1, 16, ct_wait, 0)
    acc[...] = jnp.zeros_like(acc)
    loads[4].wait()

    def places(k):
        return [lax.rem(y + dy, 4) * 4 + lax.rem(x + dx, 4) for dy, dx in ROUNDS[k]]

    shifts = (1, 15, pick(c, [2, 14]))
    sends = []

    def project(k):
        spots = places(k)

        def step(q, carry):
            p = pick(q, spots)
            for g in (0, 1):
                acc[g] += jnp.dot(ct[p], cot[g, p], preferred_element_type=F32)
            return carry

        lax.fori_loop(0, 4, step, 0)

    def z1(k):
        spots = places(k)

        def step(q, carry):
            p = pick(q, spots)
            part = lax.dot_general(
                cot[0, p], w[0], (((1,), (1,)), ((), ())), preferred_element_type=F32
            )
            part += lax.dot_general(
                cot[1, p], w[1], (((1,), (1,)), ((), ())), preferred_element_type=F32
            )
            tmp[0] = part[:64]
            tmp[1] = part[64:]
            for r in range(4):
                kept[k, r, q] = tmp[c, :, r * 128 : (r + 1) * 128]
                sib_s[k, r, q] = tmp[oc, :, r * 128 : (r + 1) * 128].astype(BF16)
            return carry

        lax.fori_loop(0, 4, step, 0)
        copy = remote(sib_s.at[k], sib_r.at[k], sib_ss.at[k], sib_rs.at[k], sibling)
        copy.start()
        sends.append(copy)

    def z2(k):
        remote(sib_s.at[k], sib_r.at[k], sib_ss.at[k], sib_rs.at[k], sibling).wait_recv()

        def step(r, carry):
            total = kept[k, r] + sib_r[k, r].astype(F32)
            kept[k, r] = total
            a_s[k, r] = total.astype(BF16)
            return carry

        lax.fori_loop(0, 4, step, 0)
        for i, delta in enumerate(shifts):
            copy = remote(
                a_s.at[k, lax.rem(z + delta, 4)], a_r.at[k, i], za_s.at[k, i], za_r.at[k, i],
                along_z(delta),
            )
            copy.start()
            sends.append(copy)

    def z3(k):
        total = kept[k, r0]
        for i in range(3):
            remote(a_r.at[k, i], a_r.at[k, i], za_s.at[k, i], za_r.at[k, i], sibling).wait_recv()
            total = total + a_r[k, i].astype(F32)
        kept[k, r0] = total
        b_s[k] = total.astype(BF16)
        for i, steps in enumerate((1, 3, 2)):
            copy = remote(
                b_s.at[k, lax.rem(q0 + steps, 4)], b_r.at[k, i], zb_s.at[k, i], zb_r.at[k, i],
                along_z(4 * steps),
            )
            copy.start()
            sends.append(copy)

    def z4(k):
        total = kept[k, r0, q0]
        for i in range(3):
            remote(b_r.at[k, i], b_r.at[k, i], zb_s.at[k, i], zb_r.at[k, i], sibling).wait_recv()
            total = total + b_r[k, i].astype(F32)
        out[k, c, r0, q0] = total.astype(BF16)
        ref = out.at[k, c, r0, q0]
        for i, steps in enumerate((1, 3, 2)):
            copy = remote(ref, ref, zc_s.at[k, i], zc_r.at[k, i], along_z(4 * steps))
            copy.start()
            sends.append(copy)

    def z5(k):
        for i, steps in enumerate((1, 3, 2)):
            ref = out.at[k, c, r0, lax.rem(q0 + 4 - steps, 4)]
            remote(ref, ref, zc_s.at[k, i], zc_r.at[k, i], sibling).wait_recv()
        ref = out.at[k, c, r0]
        for i, delta in enumerate(shifts):
            copy = remote(ref, ref, zd_s.at[k, i], zd_r.at[k, i], along_z(delta))
            copy.start()
            sends.append(copy)

    def z6(k):
        for i, delta in enumerate(shifts):
            ref = out.at[k, c, lax.rem(z + 16 - delta, 4)]
            remote(ref, ref, zd_s.at[k, i], zd_r.at[k, i], sibling).wait_recv()
        ref = out.at[k, c]
        copy = remote(ref, ref, ze_s.at[k], ze_r.at[k], sibling)
        copy.start()
        sends.append(copy)

    def z7(k):
        ref = out.at[k, oc]
        remote(ref, ref, ze_s.at[k], ze_r.at[k], sibling).wait_recv()
        spots = places(k)

        def step(q, carry):
            p = pick(q, spots)
            for half in range(2):
                rows = pl.ds(pl.multiple_of(p * 128 + half * 64, 64), 64)
                for r in range(4):
                    ig[rows, r * 128 : (r + 1) * 128] = out[k, half, r, q]
            rows = pl.ds(pl.multiple_of(p * 128, 128), 128)
            pltpu.make_async_copy(ig.at[rows], ig_h.at[rows], store_sem.at[k, q]).start()
            return carry

        lax.fori_loop(0, 4, step, 0)

    def stored(k):
        spots = places(k)

        def step(q, carry):
            rows = pl.ds(pl.multiple_of(pick(q, spots) * 128, 128), 128)
            pltpu.make_async_copy(ig.at[rows], ig_h.at[rows], store_sem.at[k, q]).wait()
            return carry

        lax.fori_loop(0, 4, step, 0)

    gather.far()
    z1(0)
    z2(0)
    project(0)
    gather.cross(1)
    z1(1)
    z3(0)
    z2(1)
    project(1)
    gather.cross(3)
    z4(0)
    z3(1)
    gather.cross(2)
    gather.rest(1)
    z1(2)
    z2(2)
    project(2)
    z5(0)
    z4(1)
    gather.rest(3)
    gather.rest(2)
    project(3)

    loads[5].wait()
    loads[6].wait()
    step_value = jnp.full((1, 1), step_s[0].astype(F32), F32)
    first_fix = 1.0 - jnp.exp(step_value * math.log(beta_one))
    second_fix = 1.0 - jnp.exp(step_value * math.log(beta_two))
    for g in (0, 1):
        projected = acc[g]
        first = beta_one * m1[g] + (1.0 - beta_one) * projected
        second = beta_two * m2[g] + (1.0 - beta_two) * projected * projected
        m1[g] = first
        m2[g] = second
        norm[g, dp] = (first / first_fix / (jnp.sqrt(second / second_fix) + adam_eps)).astype(BF16)
    ngather = Gather(norm, n_full, n_half, n_sf, n_sh, x, y)
    ngather.start()
    stores = [
        pltpu.make_async_copy(m1, fn_h, load_sem.at[5]),
        pltpu.make_async_copy(m2, sn_h, load_sem.at[6]),
    ]
    for store in stores:
        store.start()

    z1(3)
    z2(3)
    z3(2)
    z6(0)
    z5(1)
    ngather.near()
    z3(3)
    z4(2)
    ngather.far()
    z7(0)
    z6(1)
    z4(3)
    z5(2)
    ngather.cross(1)
    ngather.cross(3)
    ngather.cross(2)
    z5(3)
    z7(1)
    z6(2)
    for u in (1, 3, 2):
        ngather.rest(u)

    rows = pl.ds(pl.multiple_of(dp * 512, 512), 512)
    for g in (0, 1):
        upd[g] = jnp.dot(
            basis[rows, :], norm[g].reshape(512, 896), preferred_element_type=F32
        ).astype(BF16)
        store = pltpu.make_async_copy(upd.at[g], upd_h.at[g], load_sem.at[g])
        store.start()
        stores.append(store)
    z6(3)
    z7(2)
    z7(3)

    gather.drain()
    ngather.drain()
    for copy in sends:
        copy.wait_send()

    def ct_drain(d, carry):
        ct_copy(d).wait_send()
        return carry

    lax.fori_loop(1, 16, ct_drain, 0)
    for store in stores:
        store.wait()
    for k in range(4):
        stored(k)


def local(activations, cotangent, weights, proj_basis, first_moment, second_moment, step_number):
    any_spec = pl.BlockSpec(memory_space=pl.ANY)
    dma = pltpu.SemaphoreType.DMA
    return pl.pallas_call(
        kernel,
        out_shape=(
            jax.ShapeDtypeStruct((2048, 512), BF16),
            jax.ShapeDtypeStruct((2, 512, 896), BF16),
            jax.ShapeDtypeStruct((2, 32, 896), F32),
            jax.ShapeDtypeStruct((2, 32, 896), F32),
        ),
        in_specs=[any_spec] * 6 + [pl.BlockSpec(memory_space=pltpu.SMEM)],
        out_specs=[any_spec] * 4,
        scratch_shapes=[
            pltpu.VMEM((128, 8192), BF16),
            pltpu.VMEM((8192, 512), BF16),
            pltpu.VMEM((2, 512, 896), BF16),
            pltpu.VMEM((2, 32, 896), F32),
            pltpu.VMEM((2, 32, 896), F32),
            pltpu.VMEM((2, 16, 128, 896), BF16),
            pltpu.VMEM((512, 128), BF16),
            pltpu.VMEM((16, 32, 128), BF16),
            pltpu.VMEM((2, 16, 32, 896), BF16),
            pltpu.VMEM((2, 32, 896), F32),
            pltpu.VMEM((2, 64, 512), F32),
            pltpu.VMEM((4, 4, 4, 64, 128), F32),
            pltpu.VMEM((4, 4, 4, 64, 128), BF16),
            pltpu.VMEM((4, 4, 4, 64, 128), BF16),
            pltpu.VMEM((4, 4, 4, 64, 128), BF16),
            pltpu.VMEM((4, 3, 4, 64, 128), BF16),
            pltpu.VMEM((4, 4, 64, 128), BF16),
            pltpu.VMEM((4, 3, 64, 128), BF16),
            pltpu.VMEM((4, 2, 4, 4, 64, 128), BF16),
            pltpu.VMEM((2048, 512), BF16),
            pltpu.VMEM((2, 512, 896), BF16),
            dma((7,)),
            dma((16,)), dma((16,)),
            dma((2, 16)), dma((2, 16, 2)), dma((2, 5, 2)), dma((2, 5, 2)),
            dma((2, 16)), dma((2, 16, 2)), dma((2, 5, 2)), dma((2, 5, 2)),
            dma((4,)), dma((4,)),
            dma((4, 3)), dma((4, 3)),
            dma((4, 3)), dma((4, 3)),
            dma((4, 3)), dma((4, 3)),
            dma((4, 3)), dma((4, 3)),
            dma((4,)), dma((4,)),
            dma((4, 4)),
        ],
        compiler_params=pltpu.CompilerParams(
            collective_id=0, has_side_effects=True, vmem_limit_bytes=60 << 20
        ),
        cost_estimate=pl.CostEstimate(
            flops=6_100_000_000, bytes_accessed=24_000_000, transcendentals=60_000
        ),
    )(activations, cotangent, weights, proj_basis, first_moment, second_moment, step_number)


def solution(mesh):
    return jax.shard_map(
        local,
        mesh=mesh,
        in_specs=(
            P("dp", None),
            P(None, "dp", "tensor"),
            P(None, "dp", "tensor"),
            P(),
            P(None, "dp", "tensor"),
            P(None, "dp", "tensor"),
            P(),
        ),
        out_specs=(
            P(None, "dp"),
            P(None, "dp", "tensor"),
            P(None, "dp", "tensor"),
            P(None, "dp", "tensor"),
        ),
        check_vma=False,
    )
```

time: 348 us -> 119 us (0.34)
  waiting for transfers between devices: 178 us -> 0 us
  blocking collectives: 117 us -> 0 us
  Pallas kernels: 0 us -> 112 us
  matrix products: 28.3 us -> 0 us
  between operations: 14.5 us -> 1.3 us
    psum x1 -> x0, blocking collectives: 117 us -> none  [local(): input_grad = lax.psum(local_terms, 'tensor').astype(jnp.bfloat16)]
    pallas_call x0 -> x1, Pallas kernels: none -> 112 us  [local(): pl.pallas_call(kernel, out_shape=(jax.ShapeDtypeStruct((2048, 512), BF16)...]
    reduce_scatter x1 -> x0, waiting for transfers between devices: 94.1 us -> none  [local(): lax.psum_scatter(partial_sums, 'dp', scatter_dimension=1, tiled=True)]
    all_gather x2 -> x0, waiting for transfers between devices: 83.7 us -> none  [the longest x1 83.7 us: local(): gathered = lax.all_gather(cotangent, 'dp', axis=1, tiled=True)]
    dot_general x3 -> x0, matrix products: 28.3 us -> none  [the longest x1 9.68 us: local(): jnp.einsum('gtf,gdf->td', gathered, weights, preferred_element_type=jnp.f...]
  transfers between devices with their start and end apart: 3 -> 0, of which waited for: 2 -> 0; matrix products, arithmetic and copies ran while one was open for 3% -> 0% of each run, Pallas kernels for 0% -> 0%
where the time goes in v1:
time: 119 us
  Pallas kernels  112 us (94%)
  local copies, waits for them, and re-layouts  5.79 us (5%)
  between operations  1.3 us (1%)
    pallas_call x1, Pallas kernels, local(): pl.pallas_call(kernel, out_shape=(jax.ShapeDtypeStruct((2048, 512), BF16)...  112 us
    unnamed x10, local copies, waits for them, and re-layouts  5.79 us

profile of v1, /device:TPU:1, one launch (start us, length us, event | category | flops | bytes accessed | tf_op | source)
XLA Modules:
  0.0 119.3 jit_solution(6896841450296722792)
XLA Ops:
  1.3 112.2 %shard_map.102 = (bf16[2048,512]{1,0:T(8,128)(2,1)}, bf16[2,512,896]{2,1,0:T(8,128)(2,1)}, f32[2,32,896]{2,1,0:T(8,128)}, f32[2,32,896]{2,1,0:T(8,128)}) custom-call(bf16[128,8192]{1,0:T(8,128)(2,1)} %act_h.1, bf16[2,128,896]{2,1,0:T(8,128)(2,1)} %cot_h.1, bf16[2,512,896]{2,1,0:T(8,128)(2,1)} %w_h.1, bf16[8192,512]{1,0:T(8,128)(2,1)} %basis_h.1, ...), custom_call_target="tpu_custom_call" | custom-call | flops 6099999744 | bytes 24000000 | tf_op jit(solution)/shard_map/pallas_call | solution.py:450
  113.5 0.0 copy-start
  113.5 3.2 %copy.16 = bf16[2048,512]{1,0:T(8,128)(2,1)} copy(bf16[2048,512]{1,0:T(8,128)(2,1)} %get-tuple-element.8) | data formatting | bytes 4194304
  116.7 0.0 copy-done
  116.7 0.0 copy-start.2
  116.7 0.0 copy-start.1
  116.7 1.2 %copy.17 = bf16[2,512,896]{2,1,0:T(8,128)(2,1)} copy(bf16[2,512,896]{2,1,0:T(8,128)(2,1)S(1)} %copy-done) | data formatting | bytes 3670016
  117.9 0.0 copy-done.2
  117.9 0.7 copy.18
  118.6 0.0 copy-done.1
  118.6 0.7 copy.19
Async XLA Ops:
  113.5 3.2 %copy-start = (bf16[2,512,896]{2,1,0:T(8,128)(2,1)S(1)}, bf16[2,512,896]{2,1,0:T(8,128)(2,1)}, u32[]{:S(2)}) copy-start(bf16[2,512,896]{2,1,0:T(8,128)(2,1)} %get-tuple-element.9) | copy-start | bytes 5505028
  116.7 1.2 %copy-start.2 = (f32[2,32,896]{2,1,0:T(8,128)S(1)}, f32[2,32,896]{2,1,0:T(8,128)}, u32[]{:S(2)}) copy-start(f32[2,32,896]{2,1,0:T(8,128)} %get-tuple-element.10) | copy-start | bytes 688132
  116.7 1.9 %copy-start.1 = (f32[2,32,896]{2,1,0:T(8,128)S(1)}, f32[2,32,896]{2,1,0:T(8,128)}, u32[]{:S(2)}) copy-start(f32[2,32,896]{2,1,0:T(8,128)} %get-tuple-element.11) | copy-start | bytes 688132

commit v2 on v0

v2 whole, which is shorter than its diff:
```python
import functools
import math

import jax
import jax.numpy as jnp
from jax import lax
from jax.experimental import pallas as pl
from jax.experimental.pallas import tpu as pltpu
from jax.sharding import PartitionSpec as P

MESH = pl.DeviceIdType.MESH
beta_one = 0.9
beta_two = 0.999
adam_eps = 1e-08

F32 = jnp.float32
BF16 = jnp.bfloat16

ROUNDS = (
    ((0, 0), (0, 1), (0, 3), (1, 0)),
    ((3, 0), (0, 2), (2, 0), (3, 3), (3, 1)),
    ((1, 3), (1, 1)),
    ((3, 2), (1, 2), (2, 3)),
    ((2, 1), (2, 2)),
)
RELAYED = (True, True, True, False, False)
ORDER = (
    "cstart", "coords", "ct", "c030", "c010", "c130", "c110", "c103", "c101", "c003", "c001",
    "z1_0", "c020", "ctw", "pj_0", "c033", "c031", "z2_0", "c133", "c131", "z2b_0", "c013", "c011",
    "c113", "c111", "c120", "z1_2", "z3_0", "c102", "pj_2", "c002", "z1_1", "c132", "z3b_0", "z2_2",
    "c112", "c023", "c021", "z2_1", "pj_1", "c032", "z2b_2", "z4_0", "c123", "c121", "c012",
    "z2b_1", "z1_3", "c022", "z3_2", "pj_3", "z4b_0", "z3_1", "c122", "z1_4", "z3b_2", "z2_3",
    "z2_4", "z5_0", "pj_4", "nstart", "z3b_1", "z4_2", "z3_3", "z3_4", "z5b_0", "n030", "n010",
    "n130", "n110", "n103", "n101", "n003", "n001", "z4_1", "z4b_2", "n020", "n033", "n031", "n133",
    "n131", "n013", "n011", "n120", "n113", "n111", "n002", "n102", "z4_3", "n023", "n021", "z6_0",
    "n132", "n032", "n012", "z4_4", "z4b_1", "n123", "n121", "z7_0", "n112", "n022", "z5_2", "n122",
    "upd", "z5_3", "z5b_2", "z5_1", "z5_4", "z6_3", "z6_2", "z5b_1", "z7_3", "z7_2", "z6_4", "z6_1",
    "z7_4", "z7_1",
)


def remote(src, dst, send, recv, dev):
    return pltpu.make_async_remote_copy(
        src_ref=src, dst_ref=dst, send_sem=send, recv_sem=recv, device_id=dev, device_id_type=MESH
    )


class Gather:
    def __init__(self, buf, full, half, send_full, send_half, x, y):
        self.buf, self.full, self.half = buf, full, half
        self.send_full, self.send_half = send_full, send_half
        self.x, self.y = x, y
        self.rows = buf.shape[2] // 2
        self.sent = []

    def piece(self, g, u, v):
        dy, dx = (v, u) if g == 0 else (u, v)
        return lax.rem(self.y + dy, 4) * 4 + lax.rem(self.x + dx, 4)

    def device(self, g, axis, delta):
        along_x = (axis == 1) == (g == 0)
        if along_x:
            return {"dp": self.y * 4 + lax.rem(self.x + delta, 4)}
        return {"dp": lax.rem(self.y + delta, 4) * 4 + self.x}

    def send(self, g, axis, u, v, delta):
        p = self.piece(g, u, v)
        slot = 0 if axis == 1 else 1 + u
        ref = self.buf.at[g, p]
        copy = remote(
            ref, ref, self.send_full.at[g, slot, delta // 2], self.full.at[g, p],
            self.device(g, axis, delta),
        )
        copy.start()
        self.sent.append(copy)

    def relay(self, g, axis, u, v):
        off = u if axis == 1 else v
        delta, h = (3, 1) if off == 1 else (1, 0)
        p = self.piece(g, u, v)
        slot = 0 if axis == 1 else 1 + u
        ref = self.buf.at[g, p, pl.ds(h * self.rows, self.rows)]
        copy = remote(
            ref, ref, self.send_half.at[g, slot, h], self.half.at[g, p, h],
            self.device(g, axis, delta),
        )
        copy.start()
        self.sent.append(copy)

    def wait_full(self, g, u, v):
        p = self.piece(g, u, v)
        ref = self.buf.at[g, p]
        remote(
            ref, ref, self.send_full.at[g, 0, 0], self.full.at[g, p], self.device(g, 1, 1)
        ).wait_recv()

    def wait_halves(self, g, u, v):
        p = self.piece(g, u, v)
        for h in (0, 1):
            ref = self.buf.at[g, p, pl.ds(h * self.rows, self.rows)]
            remote(
                ref, ref, self.send_half.at[g, 0, 0], self.half.at[g, p, h], self.device(g, 1, 1)
            ).wait_recv()

    def start(self):
        for axis in (1, 2):
            for g in (0, 1):
                for delta in (1, 3):
                    self.send(g, axis, 0, 0, delta)

    def step(self, g, u, v):
        if 2 in (u if v == 0 else v, v):
            self.wait_halves(g, u, v)
        else:
            self.wait_full(g, u, v)
            self.relay(g, 1 if v == 0 else 2, u, v)
        if v == 0:
            for delta in (1, 3):
                self.send(g, 2, u, 0, delta)

    def drain(self):
        for copy in self.sent:
            copy.wait_send()


def pick(index, values):
    out = values[0]
    for i in range(1, len(values)):
        out = jnp.where(index == i, values[i], out)
    return out


def kernel(
    act_h, cot_h, w_h, basis_h, m1_h, m2_h, step_s,
    ig_h, norm_h, fn_h, sn_h,
    act, basis, w, m1, m2, cot, ct_own, ct, norm, acc, tmp, kept, sib_s, sib_r,
    a_s, a_r, b_s, b_r, out, ig,
    load_sem, ct_send, ct_recv, c_full, c_half, c_sf, c_sh, n_full, n_half, n_sf, n_sh,
    sib_ss, sib_rs, za_s, za_r, zb_s, zb_r, zc_s, zc_r, zd_s, zd_r, ze_s, ze_r, store_sem,
):
    dp = lax.axis_index("dp")
    tensor = lax.axis_index("tensor")
    y, x = lax.div(dp, 4), lax.rem(dp, 4)
    z, c = lax.div(tensor, 2), lax.rem(tensor, 2)
    oc = 1 - c
    up = 1 - 2 * c
    r0, q0 = lax.rem(z, 4), lax.div(z, 4)

    def along_z(delta):
        return {"tensor": lax.rem(z + delta + 16, 16) * 2 + c}

    def kind(delta):
        return lax.rem(z + delta + 4, 4)

    sibling = {"tensor": z * 2 + oc}

    loads = [
        pltpu.make_async_copy(cot_h.at[0], cot.at[0, dp], load_sem.at[0]),
        pltpu.make_async_copy(cot_h.at[1], cot.at[1, dp], load_sem.at[1]),
        pltpu.make_async_copy(act_h, act, load_sem.at[2]),
        pltpu.make_async_copy(basis_h, basis, load_sem.at[3]),
        pltpu.make_async_copy(w_h, w, load_sem.at[4]),
        pltpu.make_async_copy(m1_h, m1, load_sem.at[5]),
        pltpu.make_async_copy(m2_h, m2, load_sem.at[6]),
    ]
    for load in loads:
        load.start()

    barrier = pltpu.get_barrier_semaphore()

    def greet(d, carry):
        pl.semaphore_signal(
            barrier, inc=1, device_id={"dp": lax.rem(dp + d, 16)}, device_id_type=MESH
        )
        return carry

    lax.fori_loop(1, 16, greet, 0)
    for delta in (1, -1, 2, -2, 4, -4, 8):
        pl.semaphore_signal(barrier, inc=1, device_id=along_z(delta), device_id_type=MESH)
    pl.semaphore_signal(barrier, inc=1, device_id=sibling, device_id_type=MESH)
    pl.semaphore_wait(barrier, 23)

    gather = Gather(cot, c_full, c_half, c_sf, c_sh, x, y)
    ngather = Gather(norm, n_full, n_half, n_sf, n_sh, x, y)
    sends = []
    stores = []

    def cstart():
        loads[0].wait()
        loads[1].wait()
        gather.start()

    def coords():
        loads[2].wait()
        loads[3].wait()

        def coord_step(i, total):
            cols = pl.ds(pl.multiple_of(i * 1024, 1024), 1024)
            return total + jnp.dot(act[:, cols], basis[cols, :], preferred_element_type=F32)

        total = lax.fori_loop(0, 8, coord_step, jnp.zeros((128, 512), F32))
        ct_own[...] = total.T.astype(BF16)

    def ct_copy(d):
        to = lax.rem(dp + d, 16)
        rows = pl.ds(pl.multiple_of(to * 32, 32), 32)
        return remote(ct_own.at[rows], ct.at[dp], ct_send.at[d], ct_recv.at[dp], {"dp": to})

    def ct_go():
        def ct_start(d, carry):
            ct_copy(d).start()
            return carry

        lax.fori_loop(1, 16, ct_start, 0)
        ct[dp] = ct_own[pl.ds(pl.multiple_of(dp * 32, 32), 32), :]

    def ct_take():
        def ct_wait(d, carry):
            s = lax.rem(dp + d, 16)
            remote(ct.at[s], ct.at[s], ct_send.at[d], ct_recv.at[s], {"dp": s}).wait_recv()
            return carry

        lax.fori_loop(1, 16, ct_wait, 0)
        acc[...] = jnp.zeros_like(acc)

    def places(k):
        return [lax.rem(y + dy, 4) * 4 + lax.rem(x + dx, 4) for dy, dx in ROUNDS[k]]

    def first(k):
        return sum(len(r) for r in ROUNDS[:k])

    def project(k):
        spots = places(k)

        def step(i, carry):
            p = pick(i, spots)
            for g in (0, 1):
                acc[g] += jnp.dot(ct[p], cot[g, p], preferred_element_type=F32)
            return carry

        lax.fori_loop(0, len(spots), step, 0)

    def send(src, dst, ss, rs, dev):
        copy = remote(src, dst, ss, rs, dev)
        copy.start()
        sends.append(copy)

    def take(ref, ss, rs):
        remote(ref, ref, ss, rs, sibling).wait_recv()

    def span(k):
        return pl.ds(first(k) * 64, len(ROUNDS[k]) * 64)

    def bspan(k):
        return pl.ds(first(k) * 16, len(ROUNDS[k]) * 16)

    def chunk(k, steps):
        n = len(ROUNDS[k])
        q = lax.rem(q0 + steps + 4, 4)
        return pl.ds(pl.multiple_of(first(k) * 64 + q * (16 * n), 16), 16 * n)

    def z1(k):
        spots = places(k)

        def step(i, carry):
            p = pick(i, spots)
            part = lax.dot_general(
                cot[0, p], w[0], (((1,), (1,)), ((), ())), preferred_element_type=F32
            )
            part += lax.dot_general(
                cot[1, p], w[1], (((1,), (1,)), ((), ())), preferred_element_type=F32
            )
            tmp[0] = part[:64]
            tmp[1] = part[64:]
            rows = pl.ds(pl.multiple_of((first(k) + i) * 64, 64), 64)
            for r in range(4):
                kept[r, rows] = tmp[c, :, r * 128 : (r + 1) * 128]
                sib_s[r, rows] = tmp[oc, :, r * 128 : (r + 1) * 128].astype(BF16)
            return carry

        if k == 0:
            loads[4].wait()
        lax.fori_loop(0, len(spots), step, 0)
        rows = span(k)
        send(sib_s.at[:, rows], sib_r.at[:, rows], sib_ss.at[k], sib_rs.at[k], sibling)

    def z2(k):
        rows = span(k)
        take(sib_r.at[:, rows], sib_ss.at[k], sib_rs.at[k])

        def step(r, carry):
            kept[r, rows] = kept[r, rows] + sib_r[r, rows].astype(F32)
            return carry

        lax.fori_loop(0, 4, step, 0)
        moves = ((2 * up, up), (-up, -up)) if RELAYED[k] else ((up, up), (-up, -up), (2 * up, 2 * up))
        for i, (what, where) in enumerate(moves):
            a_s[i, rows] = kept[kind(what), rows].astype(BF16)
            send(
                a_s.at[i, rows], a_r.at[i, rows], za_s.at[k, i], za_r.at[k, i], along_z(where)
            )

    def z2b(k):
        rows = span(k)
        take(a_r.at[0, rows], za_s.at[k, 0], za_r.at[k, 0])
        a_s[2, rows] = (kept[kind(up), rows] + a_r[0, rows].astype(F32)).astype(BF16)
        send(a_s.at[2, rows], a_r.at[2, rows], za_s.at[k, 2], za_r.at[k, 2], along_z(up))

    def z3(k):
        rows, brows = span(k), bspan(k)
        total = kept[r0, rows]
        for i in (1, 2) if RELAYED[k] else (0, 1, 2):
            take(a_r.at[i, rows], za_s.at[k, i], za_r.at[k, i])
            total = total + a_r[i, rows].astype(F32)
        kept[r0, rows] = total
        moves = (
            ((2, 4 * up), (-up, -4 * up)) if RELAYED[k] else ((up, 4 * up), (-up, -4 * up), (2, 8))
        )
        for i, (what, where) in enumerate(moves):
            b_s[i, brows] = kept[r0, chunk(k, what)].astype(BF16)
            send(
                b_s.at[i, brows], b_r.at[i, brows], zb_s.at[k, i], zb_r.at[k, i], along_z(where)
            )

    def z3b(k):
        brows = bspan(k)
        take(b_r.at[0, brows], zb_s.at[k, 0], zb_r.at[k, 0])
        b_s[2, brows] = (kept[r0, chunk(k, up)] + b_r[0, brows].astype(F32)).astype(BF16)
        send(b_s.at[2, brows], b_r.at[2, brows], zb_s.at[k, 2], zb_r.at[k, 2], along_z(4 * up))

    def z4(k):
        brows = bspan(k)
        total = kept[r0, chunk(k, 0)]
        for i in (1, 2) if RELAYED[k] else (0, 1, 2):
            take(b_r.at[i, brows], zb_s.at[k, i], zb_r.at[k, i])
            total = total + b_r[i, brows].astype(F32)
        out[c, r0, chunk(k, 0)] = total.astype(BF16)
        ref = out.at[c, r0, chunk(k, 0)]
        for i, where in enumerate((4 * up, -4 * up) if RELAYED[k] else (4 * up, -4 * up, 8)):
            send(ref, ref, zc_s.at[k, i], zc_r.at[k, i], along_z(where))

    def z4b(k):
        ref = out.at[c, r0, chunk(k, -up)]
        take(ref, zc_s.at[k, 0], zc_r.at[k, 0])
        send(ref, ref, zc_s.at[k, 2], zc_r.at[k, 2], along_z(4 * up))

    def z5(k):
        for i, steps in enumerate((-up, up, 2)):
            if i > 0 or not RELAYED[k]:
                take(out.at[c, r0, chunk(k, steps)], zc_s.at[k, i], zc_r.at[k, i])
        ref = out.at[c, r0, span(k)]
        for i, where in enumerate((up, -up) if RELAYED[k] else (up, -up, 2 * up)):
            send(ref, ref, zd_s.at[k, i], zd_r.at[k, i], along_z(where))

    def z5b(k):
        ref = out.at[c, kind(-up), span(k)]
        take(ref, zd_s.at[k, 0], zd_r.at[k, 0])
        send(ref, ref, zd_s.at[k, 2], zd_r.at[k, 2], along_z(up))

    def z6(k):
        rows = span(k)
        for i, steps in enumerate((-up, up, 2)):
            if i > 0 or not RELAYED[k]:
                take(out.at[c, kind(steps), rows], zd_s.at[k, i], zd_r.at[k, i])
        ref = out.at[c, :, rows]
        send(ref, ref, ze_s.at[k], ze_r.at[k], sibling)

    def ig_copy(k, i):
        rows = pl.ds(pl.multiple_of(pick(i, places(k)) * 128, 128), 128)
        return pltpu.make_async_copy(ig.at[rows], ig_h.at[rows], store_sem.at[first(k) + i])

    def z7(k):
        take(out.at[oc, :, span(k)], ze_s.at[k], ze_r.at[k])
        spots = places(k)

        def step(i, carry):
            p = pick(i, spots)
            source = pl.ds(pl.multiple_of((first(k) + i) * 64, 64), 64)
            for half in range(2):
                rows = pl.ds(pl.multiple_of(p * 128 + half * 64, 64), 64)
                for r in range(4):
                    ig[rows, r * 128 : (r + 1) * 128] = out[half, r, source]
            ig_copy(k, i).start()
            return carry

        lax.fori_loop(0, len(spots), step, 0)

    def nstart():
        loads[5].wait()
        loads[6].wait()
        step_value = jnp.full((1, 1), step_s[0].astype(F32), F32)
        first_fix = 1.0 - jnp.exp(step_value * math.log(beta_one))
        second_fix = 1.0 - jnp.exp(step_value * math.log(beta_two))
        for g in (0, 1):
            projected = acc[g]
            first_new = beta_one * m1[g] + (1.0 - beta_one) * projected
            second_new = beta_two * m2[g] + (1.0 - beta_two) * projected * projected
            m1[g] = first_new
            m2[g] = second_new
            norm[g, dp] = (
                first_new / first_fix / (jnp.sqrt(second_new / second_fix) + adam_eps)
            ).astype(BF16)
        ngather.start()
        for ref, dst, i in ((m1, fn_h, 5), (m2, sn_h, 6)):
            store = pltpu.make_async_copy(ref, dst, load_sem.at[i])
            store.start()
            stores.append(store)

    def nstore():
        store = pltpu.make_async_copy(norm, norm_h, load_sem.at[0])
        store.start()
        stores.append(store)

    steps = dict(
        cstart=cstart, coords=coords, ct=ct_go, ctw=ct_take, nstart=nstart, upd=nstore,
        pj=project, z1=z1, z2=z2, z2b=z2b, z3=z3, z3b=z3b, z4=z4, z4b=z4b, z5=z5, z5b=z5b,
        z6=z6, z7=z7,
    )
    for name in ORDER:
        if name in steps:
            steps[name]()
        elif "_" in name:
            step, k = name.split("_")
            steps[step](int(k))
        else:
            g, u, v = (int(digit) for digit in name[1:])
            (gather if name[0] == "c" else ngather).step(g, u, v)

    gather.drain()
    ngather.drain()
    for copy in sends:
        copy.wait_send()

    def ct_drain(d, carry):
        ct_copy(d).wait_send()
        return carry

    lax.fori_loop(1, 16, ct_drain, 0)
    for store in stores:
        store.wait()
    for k in range(len(ROUNDS)):

        def stored(i, carry, k=k):
            ig_copy(k, i).wait()
            return carry

        lax.fori_loop(0, len(ROUNDS[k]), stored, 0)


def finish(ig_i, norm_i, basis_h, m1_i, m2_i, ig_o, upd_o, fn_o, sn_o, ig, norm, rows, upd, m1, m2, sem):
    dp = lax.axis_index("dp")
    pairs = []

    def move(i, src, ref, dst):
        pairs.append(
            (pltpu.make_async_copy(src, ref, sem.at[0, i]), pltpu.make_async_copy(ref, dst, sem.at[1, i]))
        )

    own = pltpu.make_async_copy(
        basis_h.at[pl.ds(pl.multiple_of(dp * 512, 512), 512)], rows, sem.at[0, 0]
    )
    halves = [
        (
            pltpu.make_async_copy(norm_i.at[g], norm.at[g], sem.at[0, 1 + g]),
            pltpu.make_async_copy(upd.at[g], upd_o.at[g], sem.at[1, 1 + g]),
        )
        for g in (0, 1)
    ]
    for j in range(4):
        part = pl.ds(j * 512, 512)
        move(3 + j, ig_i.at[part], ig.at[part], ig_o.at[part])
    move(7, m1_i, m1, fn_o)
    move(8, m2_i, m2, sn_o)
    own.start()
    halves[0][0].start()
    halves[1][0].start()
    for load, store in pairs:
        load.start()
    own.wait()
    for g, (load, store) in enumerate(halves):
        load.wait()
        upd[g] = jnp.dot(
            rows[...], norm[g].reshape(512, 896), preferred_element_type=F32
        ).astype(BF16)
        store.start()
        for pair in pairs[3 * g : 3 * g + 3]:
            pair[0].wait()
            pair[1].start()
    for load, store in halves + pairs:
        store.wait()


def local(activations, cotangent, weights, proj_basis, first_moment, second_moment, step_number):
    any_spec = pl.BlockSpec(memory_space=pl.ANY)
    dma = pltpu.SemaphoreType.DMA
    rounds = len(ROUNDS)
    moment = jax.ShapeDtypeStruct((2, 32, 896), F32)
    grad, norm, first_new, second_new = pl.pallas_call(
        kernel,
        out_shape=(
            jax.ShapeDtypeStruct((2048, 512), BF16),
            jax.ShapeDtypeStruct((2, 16, 32, 896), BF16),
            moment,
            moment,
        ),
        in_specs=[any_spec] * 6 + [pl.BlockSpec(memory_space=pltpu.SMEM)],
        out_specs=[any_spec] * 4,
        scratch_shapes=[
            pltpu.VMEM((128, 8192), BF16),
            pltpu.VMEM((8192, 512), BF16),
            pltpu.VMEM((2, 512, 896), BF16),
            pltpu.VMEM((2, 32, 896), F32),
            pltpu.VMEM((2, 32, 896), F32),
            pltpu.VMEM((2, 16, 128, 896), BF16),
            pltpu.VMEM((512, 128), BF16),
            pltpu.VMEM((16, 32, 128), BF16),
            pltpu.VMEM((2, 16, 32, 896), BF16),
            pltpu.VMEM((2, 32, 896), F32),
            pltpu.VMEM((2, 64, 512), F32),
            pltpu.VMEM((4, 1024, 128), F32),
            pltpu.VMEM((4, 1024, 128), BF16),
            pltpu.VMEM((4, 1024, 128), BF16),
            pltpu.VMEM((3, 1024, 128), BF16),
            pltpu.VMEM((3, 1024, 128), BF16),
            pltpu.VMEM((3, 256, 128), BF16),
            pltpu.VMEM((3, 256, 128), BF16),
            pltpu.VMEM((2, 4, 1024, 128), BF16),
            pltpu.VMEM((2048, 512), BF16),
            dma((7,)),
            dma((16,)), dma((16,)),
            dma((2, 16)), dma((2, 16, 2)), dma((2, 5, 2)), dma((2, 5, 2)),
            dma((2, 16)), dma((2, 16, 2)), dma((2, 5, 2)), dma((2, 5, 2)),
            dma((rounds,)), dma((rounds,)),
            dma((rounds, 3)), dma((rounds, 3)),
            dma((rounds, 3)), dma((rounds, 3)),
            dma((rounds, 3)), dma((rounds, 3)),
            dma((rounds, 3)), dma((rounds, 3)),
            dma((rounds,)), dma((rounds,)),
            dma((16,)),
        ],
        compiler_params=pltpu.CompilerParams(
            collective_id=0, has_side_effects=True, vmem_limit_bytes=60 << 20
        ),
        cost_estimate=pl.CostEstimate(
            flops=5_100_000_000, bytes_accessed=22_000_000, transcendentals=60_000
        ),
    )(activations, cotangent, weights, proj_basis, first_moment, second_moment, step_number)
    return pl.pallas_call(
        finish,
        out_shape=(
            jax.ShapeDtypeStruct((2048, 512), BF16),
            jax.ShapeDtypeStruct((2, 512, 896), BF16),
            moment,
            moment,
        ),
        in_specs=[any_spec] * 5,
        out_specs=[any_spec] * 4,
        scratch_shapes=[
            pltpu.VMEM((2048, 512), BF16),
            pltpu.VMEM((2, 16, 32, 896), BF16),
            pltpu.VMEM((512, 512), BF16),
            pltpu.VMEM((2, 512, 896), BF16),
            pltpu.VMEM((2, 32, 896), F32),
            pltpu.VMEM((2, 32, 896), F32),
            dma((2, 9)),
        ],
        compiler_params=pltpu.CompilerParams(vmem_limit_bytes=60 << 20),
        cost_estimate=pl.CostEstimate(
            flops=940_000_000, bytes_accessed=9_000_000, transcendentals=0
        ),
    )(grad, norm, proj_basis, first_new, second_new)


def solution(mesh):
    return jax.shard_map(
        local,
        mesh=mesh,
        in_specs=(
            P("dp", None),
            P(None, "dp", "tensor"),
            P(None, "dp", "tensor"),
            P(),
            P(None, "dp", "tensor"),
            P(None, "dp", "tensor"),
            P(),
        ),
        out_specs=(
            P(None, "dp"),
            P(None, "dp", "tensor"),
            P(None, "dp", "tensor"),
            P(None, "dp", "tensor"),
        ),
        check_vma=False,
    )
```

time: 348 us -> 108 us (0.31)
  waiting for transfers between devices: 178 us -> 0 us
  blocking collectives: 117 us -> 0 us
  Pallas kernels: 0 us -> 107 us
  matrix products: 28.3 us -> 0 us
  between operations: 14.5 us -> 1.29 us
  local copies, waits for them, and re-layouts: 5.09 us -> 0 us
    psum x1 -> x0, blocking collectives: 117 us -> none  [local(): input_grad = lax.psum(local_terms, 'tensor').astype(jnp.bfloat16)]
    pallas_call x0 -> x2, Pallas kernels: none -> 107 us  [the longest x1 103 us: local(): pl.pallas_call(kernel, out_shape=(jax.ShapeDtypeStruct((2048, 512), BF16)...]
    reduce_scatter x1 -> x0, waiting for transfers between devices: 94.1 us -> none  [local(): lax.psum_scatter(partial_sums, 'dp', scatter_dimension=1, tiled=True)]
    all_gather x2 -> x0, waiting for transfers between devices: 83.7 us -> none  [the longest x1 83.7 us: local(): gathered = lax.all_gather(cotangent, 'dp', axis=1, tiled=True)]
    dot_general x3 -> x0, matrix products: 28.3 us -> none  [the longest x1 9.68 us: local(): jnp.einsum('gtf,gdf->td', gathered, weights, preferred_element_type=jnp.f...]
    unnamed x7 -> x0, local copies, waits for them, and re-layouts: 5.09 us -> none
  transfers between devices with their start and end apart: 3 -> 0, of which waited for: 2 -> 0; matrix products, arithmetic and copies ran while one was open for 3% -> 0% of each run, Pallas kernels for 0% -> 0%
where the time goes in v2:
time: 108 us
  Pallas kernels  107 us (99%)
  between operations  1.29 us (1%)
    pallas_call x1, Pallas kernels, local(): pl.pallas_call(kernel, out_shape=(jax.ShapeDtypeStruct((2048, 512), BF16)...  103 us
    pallas_call x1, Pallas kernels, local(): pl.pallas_call(finish, out_shape=(jax.ShapeDtypeStruct((2048, 512), BF16)...  4.28 us

profile of v2, /device:TPU:1, one launch (start us, length us, event | category | flops | bytes accessed | tf_op | source)
XLA Modules:
  0.0 108.1 jit_solution(6007106885982162247)
XLA Ops:
  1.3 102.5 %shard_map.102 = (bf16[2048,512]{1,0:T(8,128)(2,1)}, bf16[2,16,32,896]{3,2,1,0:T(8,128)(2,1)}, f32[2,32,896]{2,1,0:T(8,128)}, f32[2,32,896]{2,1,0:T(8,128)}) custom-call(bf16[128,8192]{1,0:T(8,128)(2,1)} %act_h.1, bf16[2,128,896]{2,1,0:T(8,128)(2,1)} %cot_h.1, bf16[2,512,896]{2,1,0:T(8,128)(2,1)} %w_h.1, bf16[8192,512]{1,0:T(8,128)(2,1)} %basis_h.3, ...), custom_call_target="tpu_custom_call" | custom-call | flops 5100000256 | bytes 22000000 | tf_op jit(solution)/shard_map/pallas_call | solution.py:498
  103.8 4.3 %shard_map.103 = (bf16[2048,512]{1,0:T(8,128)(2,1)}, bf16[2,512,896]{2,1,0:T(8,128)(2,1)}, f32[2,32,896]{2,1,0:T(8,128)}, f32[2,32,896]{2,1,0:T(8,128)}) custom-call(bf16[2048,512]{1,0:T(8,128)(2,1)} %get-tuple-element.8.ig_i, bf16[2,16,32,896]{3,2,1,0:T(8,128)(2,1)} %get-tuple-element.9.norm_i, bf16[8192,512]{1,0:T(8,128)(2,1)} %basis_h.3, ...), custom_call_target="tpu_custom_call" | custom-call | flops 940000000 | bytes 9000000 | tf_op jit(solution)/shard_map/pallas_call | solution.py:548

commit v3 on v2

--- a/solution.py
+++ b/solution.py
@@ -16,26 +16,28 @@
 F32 = jnp.float32
 BF16 = jnp.bfloat16
 
+PARTNERS = (1, -1, 2, -2, 4, -4, 8)
 ROUNDS = (
-    ((0, 0), (0, 1), (0, 3), (1, 0)),
-    ((3, 0), (0, 2), (2, 0), (3, 3), (3, 1)),
-    ((1, 3), (1, 1)),
-    ((3, 2), (1, 2), (2, 3)),
-    ((2, 1), (2, 2)),
+    ((0, 0), (0, 1), (0, 3), (1, 0), (3, 0)),
+    ((0, 2), (2, 0), (3, 3)),
+    ((3, 1), (1, 3), (1, 1)),
+    ((3, 2), (1, 2)),
+    ((2, 3), (2, 1)),
+    ((2, 2),),
 )
-RELAYED = (True, True, True, False, False)
+RELAYED = (True, True, True, False, False, False)
 ORDER = (
     "cstart", "coords", "ct", "c030", "c010", "c130", "c110", "c103", "c101", "c003", "c001",
-    "z1_0", "c020", "ctw", "pj_0", "c033", "c031", "z2_0", "c133", "c131", "z2b_0", "c013", "c011",
-    "c113", "c111", "c120", "z1_2", "z3_0", "c102", "pj_2", "c002", "z1_1", "c132", "z3b_0", "z2_2",
-    "c112", "c023", "c021", "z2_1", "pj_1", "c032", "z2b_2", "z4_0", "c123", "c121", "c012",
-    "z2b_1", "z1_3", "c022", "z3_2", "pj_3", "z4b_0", "z3_1", "c122", "z1_4", "z3b_2", "z2_3",
-    "z2_4", "z5_0", "pj_4", "nstart", "z3b_1", "z4_2", "z3_3", "z3_4", "z5b_0", "n030", "n010",
-    "n130", "n110", "n103", "n101", "n003", "n001", "z4_1", "z4b_2", "n020", "n033", "n031", "n133",
-    "n131", "n013", "n011", "n120", "n113", "n111", "n002", "n102", "z4_3", "n023", "n021", "z6_0",
-    "n132", "n032", "n012", "z4_4", "z4b_1", "n123", "n121", "z7_0", "n112", "n022", "z5_2", "n122",
-    "upd", "z5_3", "z5b_2", "z5_1", "z5_4", "z6_3", "z6_2", "z5b_1", "z7_3", "z7_2", "z6_4", "z6_1",
-    "z7_4", "z7_1",
+    "z1_0", "c020", "ctw", "pj_0", "c033", "c031", "z2_0", "c133", "c131", "c013", "c011", "z2b_0",
+    "c113", "c111", "c120", "z1_2", "z3_0", "c102", "c002", "pj_2", "z2_2", "c132", "z1_1", "z3b_0",
+    "c112", "c023", "c021", "pj_1", "z2b_2", "z2_1", "c032", "z1_3", "z4_0", "c123", "c121", "c012",
+    "z3_2", "z2b_1", "pj_3", "z2_3", "c022", "z1_4", "pj_4", "c122", "z4b_0", "z3b_2", "z3_1",
+    "z2_4", "z1_5", "z3_3", "pj_5", "nstart", "z5_0", "z3b_1", "z4_2", "z2_5", "z3_4", "n030",
+    "n010", "n130", "n110", "n103", "n101", "n003", "n001", "z4_3", "z4_1", "n020", "n033", "n031",
+    "z3_5", "n133", "n131", "n013", "n011", "z5b_0", "n120", "n113", "n111", "n002", "n102",
+    "z4b_2", "z4_4", "n023", "n021", "n132", "n032", "z4b_1", "n012", "z5_3", "z6_0", "n123",
+    "n121", "n112", "z4_5", "z5_2", "n022", "z7_0", "z5_1", "n122", "upd", "z5_4", "z6_3", "z5b_2",
+    "z5b_1", "z7_3", "z5_5", "z6_4", "z6_2", "z6_1", "z7_4", "z6_5", "z7_2", "z7_1", "z7_5",
 )
 
 
@@ -131,12 +133,12 @@
 
 
 def kernel(
-    act_h, cot_h, w_h, basis_h, m1_h, m2_h, step_s,
+    act_h, cot_h, w_h, basis_h, m1_h, m2_h, step_h,
     ig_h, norm_h, fn_h, sn_h,
     act, basis, w, m1, m2, cot, ct_own, ct, norm, acc, tmp, kept, sib_s, sib_r,
     a_s, a_r, b_s, b_r, out, ig,
     load_sem, ct_send, ct_recv, c_full, c_half, c_sf, c_sh, n_full, n_half, n_sf, n_sh,
-    sib_ss, sib_rs, za_s, za_r, zb_s, zb_r, zc_s, zc_r, zd_s, zd_r, ze_s, ze_r, store_sem,
+    sib_ss, sib_rs, za_s, za_r, zb_s, zb_r, zc_s, zc_r, zd_s, zd_r, ze_s, ze_r, store_sem, z_ready, step_s,
 ):
     dp = lax.axis_index("dp")
     tensor = lax.axis_index("tensor")
@@ -162,6 +164,7 @@
         pltpu.make_async_copy(w_h, w, load_sem.at[4]),
         pltpu.make_async_copy(m1_h, m1, load_sem.at[5]),
         pltpu.make_async_copy(m2_h, m2, load_sem.at[6]),
+        pltpu.make_async_copy(step_h, step_s, load_sem.at[7]),
     ]
     for load in loads:
         load.start()
@@ -175,10 +178,22 @@
         return carry
 
     lax.fori_loop(1, 16, greet, 0)
-    for delta in (1, -1, 2, -2, 4, -4, 8):
-        pl.semaphore_signal(barrier, inc=1, device_id=along_z(delta), device_id_type=MESH)
     pl.semaphore_signal(barrier, inc=1, device_id=sibling, device_id_type=MESH)
-    pl.semaphore_wait(barrier, 23)
+    below = 0
+    for delta in PARTNERS:
+        above = lax.rem(z + delta + 16, 16) > z
+        below = below + jnp.where(above, 0, 1)
+
+        @pl.when(above)
+        def _(delta=delta):
+            pl.semaphore_signal(barrier, inc=1, device_id=along_z(delta), device_id_type=MESH)
+
+    pl.semaphore_wait(barrier, 16 + below)
+    for delta in PARTNERS:
+
+        @pl.when(lax.rem(z + delta + 16, 16) < z)
+        def _(delta=delta):
+            pl.semaphore_signal(z_ready, inc=1, device_id=along_z(delta), device_id_type=MESH)
 
     gather = Gather(cot, c_full, c_half, c_sf, c_sh, x, y)
     ngather = Gather(norm, n_full, n_half, n_sf, n_sh, x, y)
@@ -285,6 +300,12 @@
         send(sib_s.at[:, rows], sib_r.at[:, rows], sib_ss.at[k], sib_rs.at[k], sibling)
 
     def z2(k):
+        if ORDER.index(f"z2_{k}") == min(ORDER.index(f"z2_{j}") for j in range(len(ROUNDS))):
+
+            @pl.when(below < len(PARTNERS))
+            def _():
+                pl.semaphore_wait(z_ready, len(PARTNERS) - below)
+
         rows = span(k)
         take(sib_r.at[:, rows], sib_ss.at[k], sib_rs.at[k])
 
@@ -388,6 +409,7 @@
     def nstart():
         loads[5].wait()
         loads[6].wait()
+        loads[7].wait()
         step_value = jnp.full((1, 1), step_s[0].astype(F32), F32)
         first_fix = 1.0 - jnp.exp(step_value * math.log(beta_one))
         second_fix = 1.0 - jnp.exp(step_value * math.log(beta_two))
@@ -473,8 +495,10 @@
     move(8, m2_i, m2, sn_o)
     own.start()
     halves[0][0].start()
+    for load, store in pairs[:2]:
+        load.start()
     halves[1][0].start()
-    for load, store in pairs:
+    for load, store in pairs[2:]:
         load.start()
     own.wait()
     for g, (load, store) in enumerate(halves):
@@ -483,7 +507,7 @@
             rows[...], norm[g].reshape(512, 896), preferred_element_type=F32
         ).astype(BF16)
         store.start()
-        for pair in pairs[3 * g : 3 * g + 3]:
+        for pair in pairs[2 * g : 2 * g + 2] if g == 0 else pairs[2:]:
             pair[0].wait()
             pair[1].start()
     for load, store in halves + pairs:
@@ -503,7 +527,7 @@
             moment,
             moment,
         ),
-        in_specs=[any_spec] * 6 + [pl.BlockSpec(memory_space=pltpu.SMEM)],
+        in_specs=[any_spec] * 6 + [pl.BlockSpec(memory_space=pltpu.HBM)],
         out_specs=[any_spec] * 4,
         scratch_shapes=[
             pltpu.VMEM((128, 8192), BF16),
@@ -526,7 +550,7 @@
             pltpu.VMEM((3, 256, 128), BF16),
             pltpu.VMEM((2, 4, 1024, 128), BF16),
             pltpu.VMEM((2048, 512), BF16),
-            dma((7,)),
+            dma((8,)),
             dma((16,)), dma((16,)),
             dma((2, 16)), dma((2, 16, 2)), dma((2, 5, 2)), dma((2, 5, 2)),
             dma((2, 16)), dma((2, 16, 2)), dma((2, 5, 2)), dma((2, 5, 2)),
@@ -537,6 +561,8 @@
             dma((rounds, 3)), dma((rounds, 3)),
             dma((rounds,)), dma((rounds,)),
             dma((16,)),
+            pltpu.SemaphoreType.REGULAR,
+            pltpu.SMEM((1,), jnp.int32),
         ],
         compiler_params=pltpu.CompilerParams(
             collective_id=0, has_side_effects=True, vmem_limit_bytes=60 << 20

time: 108 us -> 105 us (0.972)
  Pallas kernels: 107 us -> 103 us
    pallas_call x1, Pallas kernels: 103 us -> 99.1 us  [local(): pl.pallas_call(kernel, out_shape=(jax.ShapeDtypeStruct((2048, 512), BF16)...]
where the time goes in v3:
time: 105 us
  Pallas kernels  103 us (98%)
  between operations  1.29 us (1%)
    pallas_call x1, Pallas kernels, local(): pl.pallas_call(kernel, out_shape=(jax.ShapeDtypeStruct((2048, 512), BF16)...  99.1 us
    pallas_call x1, Pallas kernels, local(): pl.pallas_call(finish, out_shape=(jax.ShapeDtypeStruct((2048, 512), BF16)...  4.35 us

profile of v3, /device:TPU:1, one launch (start us, length us, event | category | flops | bytes accessed | tf_op | source)
XLA Modules:
  0.0 104.8 jit_solution(9374839627482076007)
XLA Ops:
  1.3 99.1 %shard_map.102 = (bf16[2048,512]{1,0:T(8,128)(2,1)}, bf16[2,16,32,896]{3,2,1,0:T(8,128)(2,1)}, f32[2,32,896]{2,1,0:T(8,128)}, f32[2,32,896]{2,1,0:T(8,128)}) custom-call(bf16[128,8192]{1,0:T(8,128)(2,1)} %act_h.1, bf16[2,128,896]{2,1,0:T(8,128)(2,1)} %cot_h.1, bf16[2,512,896]{2,1,0:T(8,128)(2,1)} %w_h.1, bf16[8192,512]{1,0:T(8,128)(2,1)} %basis_h.3, ...), custom_call_target="tpu_custom_call" | custom-call | flops 5100000256 | bytes 22000000 | tf_op jit(solution)/shard_map/pallas_call | solution.py:522
  100.4 4.3 %shard_map.103 = (bf16[2048,512]{1,0:T(8,128)(2,1)}, bf16[2,512,896]{2,1,0:T(8,128)(2,1)}, f32[2,32,896]{2,1,0:T(8,128)}, f32[2,32,896]{2,1,0:T(8,128)}) custom-call(bf16[2048,512]{1,0:T(8,128)(2,1)} %get-tuple-element.8.ig_i, bf16[2,16,32,896]{3,2,1,0:T(8,128)(2,1)} %get-tuple-element.9.norm_i, bf16[8192,512]{1,0:T(8,128)(2,1)} %basis_h.3, ...), custom_call_target="tpu_custom_call" | custom-call | flops 940000000 | bytes 9000000 | tf_op jit(solution)/shard_map/pallas_call | solution.py:574

commit v4 on v3

--- a/solution.py
+++ b/solution.py
@@ -14,6 +14,7 @@
 adam_eps = 1e-08
 
 F32 = jnp.float32
+KERNEL_MIB = 57
 BF16 = jnp.bfloat16
 
 PARTNERS = (1, -1, 2, -2, 4, -4, 8)
@@ -134,9 +135,9 @@
 
 def kernel(
     act_h, cot_h, w_h, basis_h, m1_h, m2_h, step_h,
-    ig_h, norm_h, fn_h, sn_h,
+    ig_h, upd_h, fn_h, sn_h,
     act, basis, w, m1, m2, cot, ct_own, ct, norm, acc, tmp, kept, sib_s, sib_r,
-    a_s, a_r, b_s, b_r, out, ig,
+    a_s, a_r, b_s, b_r, out, ig, upd,
     load_sem, ct_send, ct_recv, c_full, c_half, c_sf, c_sh, n_full, n_half, n_sf, n_sh,
     sib_ss, sib_rs, za_s, za_r, zb_s, zb_r, zc_s, zc_r, zd_s, zd_r, ze_s, ze_r, store_sem, z_ready, step_s,
 ):
@@ -428,13 +429,18 @@
             store.start()
             stores.append(store)
 
-    def nstore():
-        store = pltpu.make_async_copy(norm, norm_h, load_sem.at[0])
-        store.start()
-        stores.append(store)
+    def update():
+        rows = pl.ds(pl.multiple_of(dp * 512, 512), 512)
+        for g in (0, 1):
+            upd[g] = jnp.dot(
+                basis[rows, :], norm[g].reshape(512, 896), preferred_element_type=F32
+            ).astype(BF16)
+            store = pltpu.make_async_copy(upd.at[g], upd_h.at[g], load_sem.at[g])
+            store.start()
+            stores.append(store)
 
     steps = dict(
-        cstart=cstart, coords=coords, ct=ct_go, ctw=ct_take, nstart=nstart, upd=nstore,
+        cstart=cstart, coords=coords, ct=ct_go, ctw=ct_take, nstart=nstart, upd=update,
         pj=project, z1=z1, z2=z2, z2b=z2b, z3=z3, z3b=z3b, z4=z4, z4b=z4b, z5=z5, z5b=z5b,
         z6=z6, z7=z7,
     )
@@ -469,49 +475,14 @@
         lax.fori_loop(0, len(ROUNDS[k]), stored, 0)
 
 
-def finish(ig_i, norm_i, basis_h, m1_i, m2_i, ig_o, upd_o, fn_o, sn_o, ig, norm, rows, upd, m1, m2, sem):
-    dp = lax.axis_index("dp")
-    pairs = []
-
-    def move(i, src, ref, dst):
-        pairs.append(
-            (pltpu.make_async_copy(src, ref, sem.at[0, i]), pltpu.make_async_copy(ref, dst, sem.at[1, i]))
-        )
-
-    own = pltpu.make_async_copy(
-        basis_h.at[pl.ds(pl.multiple_of(dp * 512, 512), 512)], rows, sem.at[0, 0]
-    )
-    halves = [
-        (
-            pltpu.make_async_copy(norm_i.at[g], norm.at[g], sem.at[0, 1 + g]),
-            pltpu.make_async_copy(upd.at[g], upd_o.at[g], sem.at[1, 1 + g]),
-        )
-        for g in (0, 1)
-    ]
-    for j in range(4):
-        part = pl.ds(j * 512, 512)
-        move(3 + j, ig_i.at[part], ig.at[part], ig_o.at[part])
-    move(7, m1_i, m1, fn_o)
-    move(8, m2_i, m2, sn_o)
-    own.start()
-    halves[0][0].start()
-    for load, store in pairs[:2]:
-        load.start()
-    halves[1][0].start()
-    for load, store in pairs[2:]:
-        load.start()
-    own.wait()
-    for g, (load, store) in enumerate(halves):
-        load.wait()
-        upd[g] = jnp.dot(
-            rows[...], norm[g].reshape(512, 896), preferred_element_type=F32
-        ).astype(BF16)
-        store.start()
-        for pair in pairs[2 * g : 2 * g + 2] if g == 0 else pairs[2:]:
-            pair[0].wait()
-            pair[1].start()
-    for load, store in halves + pairs:
-        store.wait()
+def finish(ig_i, upd_i, m1_i, m2_i, ig_o, upd_o, fn_o, sn_o, sem):
+    pairs = [(ig_i.at[pl.ds(j * 512, 512)], ig_o.at[pl.ds(j * 512, 512)]) for j in range(4)]
+    pairs += [(upd_i.at[g], upd_o.at[g]) for g in range(2)] + [(m1_i, fn_o), (m2_i, sn_o)]
+    copies = [pltpu.make_async_copy(src, dst, sem.at[i]) for i, (src, dst) in enumerate(pairs)]
+    for copy in copies:
+        copy.start()
+    for copy in copies:
+        copy.wait()
 
 
 def local(activations, cotangent, weights, proj_basis, first_moment, second_moment, step_number):
@@ -519,15 +490,15 @@
     dma = pltpu.SemaphoreType.DMA
     rounds = len(ROUNDS)
     moment = jax.ShapeDtypeStruct((2, 32, 896), F32)
-    grad, norm, first_new, second_new = pl.pallas_call(
+    grad, update, first_new, second_new = pl.pallas_call(
         kernel,
         out_shape=(
-            jax.ShapeDtypeStruct((2048, 512), BF16),
-            jax.ShapeDtypeStruct((2, 16, 32, 896), BF16),
-            moment,
-            moment,
+            pltpu.VMEM((2048, 512), BF16),
+            pltpu.VMEM((2, 512, 896), BF16),
+            pltpu.VMEM((2, 32, 896), F32),
+            pltpu.VMEM((2, 32, 896), F32),
         ),
-        in_specs=[any_spec] * 6 + [pl.BlockSpec(memory_space=pltpu.HBM)],
+        in_specs=[pl.BlockSpec(memory_space=pltpu.HBM)] * 7,
         out_specs=[any_spec] * 4,
         scratch_shapes=[
             pltpu.VMEM((128, 8192), BF16),
@@ -550,6 +521,7 @@
             pltpu.VMEM((3, 256, 128), BF16),
             pltpu.VMEM((2, 4, 1024, 128), BF16),
             pltpu.VMEM((2048, 512), BF16),
+            pltpu.VMEM((2, 512, 896), BF16),
             dma((8,)),
             dma((16,)), dma((16,)),
             dma((2, 16)), dma((2, 16, 2)), dma((2, 5, 2)), dma((2, 5, 2)),
@@ -565,10 +537,10 @@
             pltpu.SMEM((1,), jnp.int32),
         ],
         compiler_params=pltpu.CompilerParams(
-            collective_id=0, has_side_effects=True, vmem_limit_bytes=60 << 20
+            collective_id=0, has_side_effects=True, vmem_limit_bytes=KERNEL_MIB << 20
         ),
         cost_estimate=pl.CostEstimate(
-            flops=5_100_000_000, bytes_accessed=22_000_000, transcendentals=60_000
+            flops=6_000_000_000, bytes_accessed=22_000_000, transcendentals=60_000
         ),
     )(activations, cotangent, weights, proj_basis, first_moment, second_moment, step_number)
     return pl.pallas_call(
@@ -579,22 +551,12 @@
             moment,
             moment,
         ),
-        in_specs=[any_spec] * 5,
+        in_specs=[any_spec] * 4,
         out_specs=[any_spec] * 4,
-        scratch_shapes=[
-            pltpu.VMEM((2048, 512), BF16),
-            pltpu.VMEM((2, 16, 32, 896), BF16),
-            pltpu.VMEM((512, 512), BF16),
-            pltpu.VMEM((2, 512, 896), BF16),
-            pltpu.VMEM((2, 32, 896), F32),
-            pltpu.VMEM((2, 32, 896), F32),
-            dma((2, 9)),
-        ],
-        compiler_params=pltpu.CompilerParams(vmem_limit_bytes=60 << 20),
-        cost_estimate=pl.CostEstimate(
-            flops=940_000_000, bytes_accessed=9_000_000, transcendentals=0
-        ),
-    )(grad, norm, proj_basis, first_new, second_new)
+        scratch_shapes=[dma((8,))],
+        compiler_params=pltpu.CompilerParams(vmem_limit_bytes=4 << 20),
+        cost_estimate=pl.CostEstimate(flops=0, bytes_accessed=4_500_000, transcendentals=0),
+    )(grad, update, first_new, second_new)
 
 
 def solution(mesh):

time: 105 us -> 102 us (0.971)
  Pallas kernels: 103 us -> 101 us
    pallas_call x1, Pallas kernels: 4.35 us -> 2.13 us  [local(): pl.pallas_call(finish, out_shape=(jax.ShapeDtypeStruct((2048, 512), BF16)...]
where the time goes in v4:
time: 102 us
  Pallas kernels  101 us (99%)
  between operations  1.29 us (1%)
    pallas_call x1, Pallas kernels, local(): pl.pallas_call(kernel, out_shape=(pltpu.VMEM((2048, 512), BF16), pltpu.VM...  98.9 us
    pallas_call x1, Pallas kernels, local(): pl.pallas_call(finish, out_shape=(jax.ShapeDtypeStruct((2048, 512), BF16)...  2.13 us

profile of v4, /device:TPU:1, one launch (start us, length us, event | category | flops | bytes accessed | tf_op | source)
XLA Modules:
  0.0 102.3 jit_solution(11020243075683932829)
XLA Ops:
  1.3 98.9 %shard_map.102 = (bf16[2048,512]{1,0:T(8,128)(2,1)S(1)}, bf16[2,512,896]{2,1,0:T(8,128)(2,1)S(1)}, f32[2,32,896]{2,1,0:T(8,128)S(1)}, f32[2,32,896]{2,1,0:T(8,128)S(1)}) custom-call(bf16[128,8192]{1,0:T(8,128)(2,1)} %act_h.1, bf16[2,128,896]{2,1,0:T(8,128)(2,1)} %cot_h.1, bf16[2,512,896]{2,1,0:T(8,128)(2,1)} %w_h.1, bf16[8192,512]{1,0:T(8,128)(2,1)} %basis_h.1, ...), custom_call_target="tpu_custom_call" | custom-call | flops 6000000000 | bytes 22000000 | tf_op jit(solution)/shard_map/pallas_call | solution.py:493
  100.2 2.1 %shard_map.103 = (bf16[2048,512]{1,0:T(8,128)(2,1)}, bf16[2,512,896]{2,1,0:T(8,128)(2,1)}, f32[2,32,896]{2,1,0:T(8,128)}, f32[2,32,896]{2,1,0:T(8,128)}) custom-call(bf16[2048,512]{1,0:T(8,128)(2,1)S(1)} %get-tuple-element.8.ig_i, bf16[2,512,896]{2,1,0:T(8,128)(2,1)S(1)} %get-tuple-element.9.upd_i, f32[2,32,896]{2,1,0:T(8,128)S(1)} %get-tuple-element.10.m1_i, ...), custom_call_target="tpu_custom_call" | custom-call | bytes 4500000 | tf_op jit(solution)/shard_map/pallas_call | solution.py:546

commit v5 on v4

--- a/solution.py
+++ b/solution.py
@@ -310,17 +310,17 @@
         rows = span(k)
         take(sib_r.at[:, rows], sib_ss.at[k], sib_rs.at[k])
 
-        def step(r, carry):
-            kept[r, rows] = kept[r, rows] + sib_r[r, rows].astype(F32)
-            return carry
-
-        lax.fori_loop(0, 4, step, 0)
+        def total(r):
+            return kept[r, rows] + sib_r[r, rows].astype(F32)
+
         moves = ((2 * up, up), (-up, -up)) if RELAYED[k] else ((up, up), (-up, -up), (2 * up, 2 * up))
         for i, (what, where) in enumerate(moves):
-            a_s[i, rows] = kept[kind(what), rows].astype(BF16)
+            a_s[i, rows] = total(kind(what)).astype(BF16)
             send(
                 a_s.at[i, rows], a_r.at[i, rows], za_s.at[k, i], za_r.at[k, i], along_z(where)
             )
+        for r in (r0, kind(up)) if RELAYED[k] else (r0,):
+            kept[r, rows] = total(r)
 
     def z2b(k):
         rows = span(k)
@@ -330,19 +330,24 @@
 
     def z3(k):
         rows, brows = span(k), bspan(k)
-        total = kept[r0, rows]
-        for i in (1, 2) if RELAYED[k] else (0, 1, 2):
+        parts = (1, 2) if RELAYED[k] else (0, 1, 2)
+        for i in parts:
             take(a_r.at[i, rows], za_s.at[k, i], za_r.at[k, i])
-            total = total + a_r[i, rows].astype(F32)
-        kept[r0, rows] = total
+
+        def total(steps):
+            own = chunk(k, steps)
+            return sum((a_r[i, own].astype(F32) for i in parts), kept[r0, own])
+
         moves = (
             ((2, 4 * up), (-up, -4 * up)) if RELAYED[k] else ((up, 4 * up), (-up, -4 * up), (2, 8))
         )
         for i, (what, where) in enumerate(moves):
-            b_s[i, brows] = kept[r0, chunk(k, what)].astype(BF16)
+            b_s[i, brows] = total(what).astype(BF16)
             send(
                 b_s.at[i, brows], b_r.at[i, brows], zb_s.at[k, i], zb_r.at[k, i], along_z(where)
             )
+        for steps in (0, up) if RELAYED[k] else (0,):
+            kept[r0, chunk(k, steps)] = total(steps)
 
     def z3b(k):
         brows = bspan(k)

time: 102 us -> 102 us (level)
  no operation moved by 1% of the time
where the time goes in v5:
time: 102 us
  Pallas kernels  101 us (99%)
  between operations  1.29 us (1%)
    pallas_call x1, Pallas kernels, local(): pl.pallas_call(kernel, out_shape=(pltpu.VMEM((2048, 512), BF16), pltpu.VM...  98.5 us
    pallas_call x1, Pallas kernels, local(): pl.pallas_call(finish, out_shape=(jax.ShapeDtypeStruct((2048, 512), BF16)...  2.13 us

profile of v5, /device:TPU:1, one launch (start us, length us, event | category | flops | bytes accessed | tf_op | source)
XLA Modules:
  0.0 102.0 jit_solution(11623152281561263867)
XLA Ops:
  1.3 98.5 %shard_map.102 = (bf16[2048,512]{1,0:T(8,128)(2,1)S(1)}, bf16[2,512,896]{2,1,0:T(8,128)(2,1)S(1)}, f32[2,32,896]{2,1,0:T(8,128)S(1)}, f32[2,32,896]{2,1,0:T(8,128)S(1)}) custom-call(bf16[128,8192]{1,0:T(8,128)(2,1)} %act_h.1, bf16[2,128,896]{2,1,0:T(8,128)(2,1)} %cot_h.1, bf16[2,512,896]{2,1,0:T(8,128)(2,1)} %w_h.1, bf16[8192,512]{1,0:T(8,128)(2,1)} %basis_h.1, ...), custom_call_target="tpu_custom_call" | custom-call | flops 6000000000 | bytes 22000000 | tf_op jit(solution)/shard_map/pallas_call | solution.py:498
  99.8 2.1 %shard_map.103 = (bf16[2048,512]{1,0:T(8,128)(2,1)}, bf16[2,512,896]{2,1,0:T(8,128)(2,1)}, f32[2,32,896]{2,1,0:T(8,128)}, f32[2,32,896]{2,1,0:T(8,128)}) custom-call(bf16[2048,512]{1,0:T(8,128)(2,1)S(1)} %get-tuple-element.8.ig_i, bf16[2,512,896]{2,1,0:T(8,128)(2,1)S(1)} %get-tuple-element.9.upd_i, f32[2,32,896]{2,1,0:T(8,128)S(1)} %get-tuple-element.10.m1_i, ...), custom_call_target="tpu_custom_call" | custom-call | bytes 4500000 | tf_op jit(solution)/shard_map/pallas_call | solution.py:551
